TPU v7x, 32 devices: a whole 2x2x4 slice. The times are simulated.
32 devices in a mesh: col: 16 (over z, y, x), row: 2 (over core).
Axes of the slice: x: 2, y: 2, z: 4, core: 2. Of those that a mesh axis runs over, the one named last changes fastest.
Arguments:
- features: bfloat16 [64, 32768], P(None, ('col', 'row')), may hold values from -6 to 6
- preact: bfloat16 [64, 32768], P(None, ('col', 'row')), may hold values from -8 to 8
- coarse_grad: bfloat16 [128, 4096], P(None, ('col', 'row')), may hold values from -6 to 6
- kernel_one: bfloat16 [27, 64, 64], replicated, may hold values from -0.15625 to 0.15625
- kernel_two: bfloat16 [8, 128, 64], replicated, may hold values from -0.25 to 0.25
- neighbours: int32 [27, 32768], P(None, ('col', 'row')), may hold values from 0 to 3040, as said below
- send_list: int32 [7168], P(('col', 'row')), may hold values from 0 to 1023, as said below
- parent_slot: int32 [32768], P(('col', 'row')), may hold values from 0 to 127, as said below
- child_pos: int32 [32768], P(('col', 'row')), may hold values from 0 to 7, as said below
Outputs:
- feature_grad: bfloat16 [64, 32768], P(None, ('col', 'row'))
- kernel_one_grad: float32 [27, 64, 64], replicated
- kernel_two_grad: float32 [8, 128, 64], replicated
Inputs may be any that keep to these rules, and one draw needn't show every extreme that they name: Entries come from the geometry of occupied fine voxels in 16 x 16 x (256) columns, one column a device: neighbour relations are mutual (N(i, o) = j exactly when N(j, 26 - o) = i), entries of 3040 mark empty neighbours, and remote entries only name devices beside the holder along col and row. `send_list`: distinct voxels of the holding device, exactly those that lie on the outermost fine layer of its column along x or y. `parent_slot`: the coarse level is spread over col by a load hash: every value names the parent of exactly 8 fine voxels of the device, so each device along col owns 8 parents of each device of the same row index. `child_pos`: the 8 children of a parent have distinct positions.
All inputs are finite; a program needn't handle non-finite values.
Results may differ from a plain program's by a relative error of at most 0.0049.
Values may be sent and summed in bfloat16 or wider, within the bound.
A program may use at most 64 MiB of HBM per device.

v0:
```python
import jax
import jax.numpy as jnp
from jax import lax
from jax.sharding import PartitionSpec as P


def extended(block, sides, width):
    for axis, dim in sides:
        count = lax.axis_size(axis)
        forward = [(i, i + 1) for i in range(count - 1)]
        backward = [(target, source) for source, target in forward]
        low = lax.ppermute(
            lax.slice_in_dim(block, block.shape[dim] - width, None, axis=dim), axis, forward
        )
        high = lax.ppermute(lax.slice_in_dim(block, 0, width, axis=dim), axis, backward)
        block = jnp.concatenate([low, block, high], axis=dim)
    return block


def body(
    features,
    preact,
    coarse_grad,
    kernel_one,
    kernel_two,
    neighbours,
    send_list,
    parent_slot,
    child_pos,
):
    channels, sites = features.shape
    n_col = lax.axis_size("col")
    owners_grad = lax.all_to_all(coarse_grad, "col", split_axis=1, concat_axis=1, tiled=True)
    parent_grad = jnp.take(owners_grad, parent_slot, axis=1)
    pre = preact.astype(jnp.float32)
    gate_sig = jax.nn.sigmoid(pre)
    act = (pre * gate_sig).astype(jnp.bfloat16)
    onehot = child_pos[None, :] == jnp.arange(8, dtype=jnp.int32)[:, None]
    stacked_prod = jnp.einsum(
        "kcd,cs->kds", kernel_two, parent_grad, preferred_element_type=jnp.float32
    )
    act_grad = jnp.sum(jnp.where(onehot[:, None, :], stacked_prod, 0.0), axis=0)
    pre_grad = (act_grad * gate_sig * (1.0 + pre * (1.0 - gate_sig))).astype(jnp.bfloat16)
    masked = jnp.where(onehot[:, None, :], act[None, :, :], jnp.zeros((), jnp.bfloat16))
    two_part = jnp.einsum("cs,kds->kcd", parent_grad, masked, preferred_element_type=jnp.float32)
    stacked = jnp.concatenate([features, pre_grad], axis=0)
    offered = jnp.take(stacked, send_list, axis=1)[:, None, None, :]
    beside_all = extended(offered, (("col", 1), ("row", 2)), 1)
    remote_cols = beside_all.reshape(2 * channels, 9 * send_list.shape[0])
    zero_cols = jnp.zeros((2 * channels, 128), jnp.bfloat16)
    table = jnp.concatenate([stacked, remote_cols, zero_cols], axis=1)
    feat_table = table[:channels]
    grad_table = table[channels:]

    def per_offset(carry, pieces):
        near, mirror, weight = pieces
        near_feat = jnp.take(feat_table, near, axis=1)
        grad_w = lax.dot_general(
            pre_grad, near_feat, (((1,), (1,)), ((), ())), preferred_element_type=jnp.float32
        )
        near_grad = jnp.take(grad_table, mirror, axis=1)
        carry = carry + lax.dot_general(
            weight, near_grad, (((0,), (0,)), ((), ())), preferred_element_type=jnp.float32
        )
        return (carry, grad_w)

    feat_grad, one_part = lax.scan(
        per_offset,
        jnp.zeros((channels, sites), jnp.float32),
        (neighbours, neighbours[::-1], kernel_one),
    )
    one_sum, two_sum = lax.psum((one_part, two_part), ("col", "row"))
    scale = float(sites * n_col * lax.axis_size("row")) ** (-0.5)
    return (feat_grad.astype(jnp.bfloat16), one_sum * scale, two_sum * scale)


def solution(mesh):
    placed = (
        P(None, ("col", "row")),
        P(None, ("col", "row")),
        P(None, ("col", "row")),
        P(),
        P(),
        P(None, ("col", "row")),
        P(("col", "row")),
        P(("col", "row")),
        P(("col", "row")),
    )
    return jax.shard_map(
        body,
        mesh=mesh,
        in_specs=placed,
        out_specs=(P(None, ("col", "row")), P(), P()),
        check_vma=False,
    )
```

profile of v0, /device:TPU:0, one launch (start us, length us, event | category | flops | bytes accessed | tf_op | source)
XLA Modules:
  0.0 422.0 jit_solution(2362267887494416250)
XLA Ops:
  8.7 8.3 %all-to-all-start = ((bf16[128,16,8]{0,2,1:T(8,128)(2,1)}), bf16[128,16,8]{0,2,1:T(8,128)(2,1)S(1)}, u32[]{:S(2)}, u32[]{:S(2)}) async-start(bf16[128,16,8]{0,2,1:T(8,128)(2,1)} %bitcast), calls=%async_computation | async-start | bytes 65536 | tf_op jit(solution)/shard_map/all_to_all | solution.py:33
  20.5 3.9 all-to-all-done
  31.6 4.5 %collective-permute-start = (bf16[128,1,1,224]{0,3,2,1:T(8,128)(2,1)S(1)}, bf16[128,1,1,224]{0,3,2,1:T(8,128)(2,1)S(1)}, u32[]{:S(2)}, u32[]{:S(2)}) collective-permute-start(bf16[128,1,1,224]{0,3,2,1:T(8,128)(2,1)S(1)} %bitcast_select_fusion), channel_id=1, source_target_pairs={{0,2},{2,4},{4,6},{6,8},{8,10},{10,12},{12,14},{14,16},{16,18},{18... | collective-permute-start | bytes 172040 | tf_op jit(solution)/shard_map/ppermute | solution.py:12
  44.4 235.5 %while.13 = (s32[]{:T(128)}, f32[64,1024]{1,0:T(8,128)S(1)}, f32[27,64,64]{2,1,0:T(8,128)}, bf16[27,64,64]{2,1,0:T(8,128)(2,1)}, s32[27,1024]{1,0:T(8,128)S(1)},...) while((s32[]{:T(128)}, f32[64,1024]{1,0:T(8,128)S(1)}, ...), condition=%wide.region_2.4_spmd.clone, body=%wide.region_1.3_spmd.clone.sunk | while | flops 17059844 | bytes 1609867 | solution.py:67
  48.9 3.2 gather_fusion.1
  57.6 3.2 gather_fusion.1
  66.3 3.2 gather_fusion.1
  75.0 3.2 gather_fusion.1
  92.5 3.2 gather_fusion.1
  109.9 3.2 gather_fusion.1
  118.6 3.2 gather_fusion.1
  127.4 3.2 gather_fusion.1
  136.1 3.2 gather_fusion.1
  144.8 3.2 gather_fusion.1
  153.5 3.2 gather_fusion.1
  179.7 3.2 gather_fusion.1
  197.1 3.2 gather_fusion.1
  205.9 3.2 gather_fusion.1
  214.6 3.2 gather_fusion.1
  223.3 3.2 gather_fusion.1
  240.8 3.2 gather_fusion.1
  249.5 3.2 gather_fusion.1
  258.2 3.2 gather_fusion.1
  280.7 130.6 %all-reduce.3.cloned.1.call-done = (f32[27,64,64]{2,1,0:T(8,128)}, f32[8,128,64]{1,2,0:T(8,128)}) async-done(((f32[27,64,64]{2,1,0:T(8,128)}, f32[8,128,64]{1,2,0:T(8,128)}), (f32[27,64,64]{2,1,0:T(8,128)}, f32[8,128,64]{1,2,0:T(8,128)})) %all-reduce.3.cloned.1.call-update) | async-done | bytes 704528 | tf_op jit(solution)/shard_map/psum | solution.py:72
  (323 shorter events, 197.7 us)
Async XLA Ops:
  7.2 20.5 %copy-start = (bf16[8,128,64]{1,2,0:T(8,128)(2,1)S(1)}, bf16[8,128,64]{1,2,0:T(8,128)(2,1)}, u32[]{:S(2)}) copy-start(bf16[8,128,64]{1,2,0:T(8,128)(2,1)} %param.17) | copy-start | bytes 393220
  8.7 15.7 %all-to-all-start = ((bf16[128,16,8]{0,2,1:T(8,128)(2,1)}), bf16[128,16,8]{0,2,1:T(8,128)(2,1)S(1)}, u32[]{:S(2)}, u32[]{:S(2)}) async-start(bf16[128,16,8]{0,2,1:T(8,128)(2,1)} %bitcast), calls=%async_computation | async-start | bytes 65536 | tf_op jit(solution)/shard_map/all_to_all | solution.py:33
  17.0 394.2 %all-reduce.3.cloned.1.call-start = ((), (), s32[]{:S(2)}) async-start(), calls=%async_computation.1 | async-start | bytes 2293760 | tf_op jit(solution)/shard_map/psum | solution.py:72
  27.6 0.9 copy-start.2
  28.2 0.9 copy-start.3
  28.2 7.9 %copy-start.1 = (s32[27,1024]{1,0:T(8,128)S(1)}, s32[27,1024]{1,0:T(8,128)}, u32[]{:S(2)}) copy-start(s32[27,1024]{1,0:T(8,128)} %param.18) | copy-start | bytes 331780
  30.3 6.2 %collective-permute-start.1 = (bf16[128,1,1,224]{0,3,2,1:T(8,128)(2,1)S(1)}, bf16[128,1,1,224]{0,3,2,1:T(8,128)(2,1)S(1)}, u32[]{:S(2)}, u32[]{:S(2)}) collective-permute-start(bf16[128,1,1,224]{0,3,2,1:T(8,128)(2,1)S(1)} %bitcast_select_fusion), channel_id=1, source_target_pairs={{2,0},{4,2},{6,4},{8,6},{10,8},{12,10},{14,12},{16,14},{18,16},{20... | collective-permute-start | bytes 172040 | tf_op jit(solution)/shard_map/ppermute | solution.py:15
  31.6 6.4 %collective-permute-start = (bf16[128,1,1,224]{0,3,2,1:T(8,128)(2,1)S(1)}, bf16[128,1,1,224]{0,3,2,1:T(8,128)(2,1)S(1)}, u32[]{:S(2)}, u32[]{:S(2)}) collective-permute-start(bf16[128,1,1,224]{0,3,2,1:T(8,128)(2,1)S(1)} %bitcast_select_fusion), channel_id=1, source_target_pairs={{0,2},{2,4},{4,6},{6,8},{8,10},{10,12},{12,14},{14,16},{16,18},{18... | collective-permute-start | bytes 172040 | tf_op jit(solution)/shard_map/ppermute | solution.py:12
  37.9 5.6 %collective-permute-start.3 = (bf16[128,3,1,224]{0,3,2,1:T(8,128)(2,1)S(1)}, bf16[128,3,1,224]{0,3,2,1:T(8,128)(2,1)S(1)}, u32[]{:S(2)}, u32[]{:S(2)}) collective-permute-start(bf16[128,3,1,224]{0,3,2,1:T(8,128)(2,1)S(1)} %pad_maximum_fusion.2), channel_id=1, source_target_pairs={{1,0},{3,2},{5,4},{7,6},{9,8},{11,10},{13,12},{15,14},{17,16},{19,... | collective-permute-start | bytes 516104 | tf_op jit(solution)/shard_map/ppermute | solution.py:15
  39.2 4.3 %collective-permute-start.2 = (bf16[128,3,1,224]{0,3,2,1:T(8,128)(2,1)S(1)}, bf16[128,3,1,224]{0,3,2,1:T(8,128)(2,1)S(1)}, u32[]{:S(2)}, u32[]{:S(2)}) collective-permute-start(bf16[128,3,1,224]{0,3,2,1:T(8,128)(2,1)S(1)} %pad_maximum_fusion.2), channel_id=1, source_target_pairs={{0,1},{2,3},{4,5},{6,7},{8,9},{10,11},{12,13},{14,15},{16,17},{18,... | collective-permute-start | bytes 516104 | tf_op jit(solution)/shard_map/ppermute | solution.py:12
Sparse Core Ops, SparseCore 0:
  280.1 131.0 all-reduce.2
where the time goes:
time: 425 us; the launch traced here: 422 us
  local copies, waits for them, and re-layouts  199 us (47%)
  waiting for transfers between devices  136 us (32%)
  matrix products  42.3 us (10%)
  starting transfers between devices  18.5 us (4%)
  between operations  14.2 us (3%)
  other arithmetic  9.83 us (2%)
    psum x1, waiting for transfers between devices, body(): one_sum, two_sum = lax.psum((one_part, two_part), ('col', 'row'))  131 us
    gather x27, local copies, waits for them, and re-layouts, per_offset(): near_feat = jnp.take(feat_table, near, axis=1)  86.7 us
    gather x27, local copies, waits for them, and re-layouts, per_offset(): near_grad = jnp.take(grad_table, mirror, axis=1)  86.6 us
    dot_general x27, matrix products, per_offset(): lax.dot_general(weight, near_grad, (((0,), (0,)), ((), ())), preferred_el...  30.3 us
    dynamic_update_slice x54, local copies, waits for them, and re-layouts, body(): lax.scan(per_offset, jnp.zeros((channels, sites), jnp.float32), (neighbou...  19.1 us
    dot_general x27, matrix products, per_offset(): lax.dot_general(pre_grad, near_feat, (((1,), (1,)), ((), ())), preferred_...  10.2 us
  transfers between devices with their start and end apart: 6, of which 3 were waited for; matrix products, arithmetic and copies ran while one was open for 1% of the time, Pallas kernels for 0%

commit v1 on v0

v1 whole, which is shorter than its diff:
```python
import functools

import jax
import jax.numpy as jnp
from jax import lax
from jax.experimental import pallas as pl
from jax.experimental.pallas import tpu as pltpu
from jax.sharding import PartitionSpec as P

F32 = jnp.float32
BF16 = jnp.bfloat16
NT = (((1,), (1,)), ((), ()))
TN = (((0,), (0,)), ((), ()))
MESH = pl.DeviceIdType.MESH
BESIDE = [(x, y) for x in (-1, 0, 1) for y in (-1, 0, 1) if (x, y) != (0, 0)]


def pick(index_row, rows):
    n = index_row.shape[1]
    spot = lax.broadcasted_iota(jnp.int32, (rows, n), 0)
    return jnp.where(spot == index_row, 1.0, 0.0).astype(BF16)


def dot(a, b, dims=(((1,), (0,)), ((), ()))):
    return lax.dot_general(a, b, dims, preferred_element_type=F32)


def remote(src, dst, send_sem, recv_sem, col, row):
    return pltpu.make_async_remote_copy(
        src_ref=src, dst_ref=dst, send_sem=send_sem, recv_sem=recv_sem,
        device_id=(col, row), device_id_type=MESH)


def others(me, count, step):
    def one(j, carry):
        step(lax.rem(me + j, count))
        return carry
    lax.fori_loop(1, count, one, 0)


def kernel(sizes, coarse_ref, slot_ref, child_ref, preact_ref, feat_ref, two_ref, one_ref, nb_ref,
           send_ref, feat_out_ref, sum_ref,
           owners, grad, offer, halo, ng, ngr, feat_two, part, row_in, mid, col_in, fin,
           coarse_sems, halo_sems, row_sems, col_sems, gather_col_sems, gather_row_sems):
    n_col, n_row, width, held, share = sizes
    channels, sites = feat_ref.shape
    offsets = nb_ref.shape[0]
    pairs = (offsets + 1) // 2
    padded = send_ref.shape[1]
    tile = 256
    c, r = lax.axis_index("col"), lax.axis_index("row")

    def beside(x, y):
        return ((c + x >= 0) & (c + x < n_col) & (r + y >= 0) & (r + y < n_row))

    barrier = pltpu.get_barrier_semaphore()

    def greet(col, row):
        pl.semaphore_signal(barrier, inc=1, device_id=(col, row), device_id_type=MESH)

    others(c, n_col, lambda peer: greet(peer, r))
    others(r, n_row, lambda peer: greet(c, peer))
    count = n_col - 1 + n_row - 1
    for x, y in BESIDE:
        if x != 0 and y != 0:
            there = beside(x, y)

            @pl.when(there)
            def _():
                greet(c + x, r + y)

            count = count + jnp.where(there, 1, 0)
    pl.semaphore_wait(barrier, count)

    def coarse_copy(src_col, dst_col, to):
        return remote(coarse_ref.at[dst_col], owners.at[src_col], coarse_sems.at[0, dst_col],
                      coarse_sems.at[1, src_col], to, r)

    others(c, n_col, lambda peer: coarse_copy(c, peer, peer).start())
    owners[pl.ds(c, 1)] = coarse_ref[pl.ds(c, 1)]
    pre = preact_ref[...].astype(F32)
    gate = jax.nn.sigmoid(pre)
    act = (pre * gate).astype(BF16).astype(F32)
    slot = slot_ref[...]
    lines = owners.shape[1]
    line = slot // held * lines + slot % held
    chosen_parent = pick(line, n_col * lines)
    child = child_ref[...]
    for x, y in BESIDE:
        @pl.when(jnp.logical_not(beside(x, y)))
        def _():
            halo[(x + 1) * 3 + y + 1] = jnp.zeros(halo.shape[1:], BF16)
    ng[pl.ds(offsets * channels, channels), :] = jnp.zeros((channels, sites), BF16)
    ngr[pl.ds(offsets * channels, channels), :] = jnp.zeros((channels, padded), BF16)
    feat_two[0, pl.ds(0, channels), :] = feat_ref[...]
    feat_two[0, pl.ds(channels, channels), :] = jnp.zeros((channels, sites), BF16)
    feat_two[1, pl.ds(0, channels), :] = jnp.zeros((channels, sites), BF16)
    feat_two[1, pl.ds(channels, channels), :] = feat_ref[...]
    others(c, n_col, lambda peer: coarse_copy(peer, c, c).wait_recv())
    all_owned = owners[...].reshape(n_col * lines, owners.shape[2])
    parent = dot(all_owned.astype(F32).T.astype(BF16), chosen_parent).astype(BF16)
    act_grad = jnp.zeros((channels, sites), F32)
    for k in range(8):
        rows = pl.ds(k * channels, channels)
        here = jnp.broadcast_to(child == k, (channels, sites))
        act_grad = jnp.where(here, dot(two_ref[rows, :], parent), act_grad)
    grad[...] = (act_grad * gate * (1.0 + pre * (1.0 - gate))).astype(BF16)
    chosen = pick(send_ref[...], sites)
    offer[...] = dot(grad[...], chosen).astype(BF16)

    def halo_copy(x, y):
        b = (x + 1) * 3 + y + 1
        return remote(offer, halo.at[8 - b], halo_sems.at[0, b], halo_sems.at[1, 8 - b],
                      c + x, r + y)

    for x, y in BESIDE:
        @pl.when(beside(x, y))
        def _():
            halo_copy(x, y).start()

    base = pairs * channels
    for k in range(8):
        here = jnp.broadcast_to(child == k, (channels, sites))
        masked = jnp.where(here, act, 0.0).astype(BF16)
        part[pl.ds(base + k * channels, channels), :] = dot(masked, parent, NT).astype(BF16)
    spare = base + 8 * channels
    if part.shape[0] > spare:
        part[pl.ds(spare, part.shape[0] - spare), :] = jnp.zeros(
            (part.shape[0] - spare, part.shape[1]), BF16)

    def near(o, carry):
        rows = pl.ds(pl.multiple_of(o * channels, channels), channels)
        for at in range(0, sites, tile):
            columns = pl.ds(at, tile)
            ng[rows, columns] = dot(
                grad[...], pick(nb_ref[pl.ds(offsets - 1 - o, 1), columns], sites)
            ).astype(BF16)
        return carry

    lax.fori_loop(0, offsets, near, 0)
    feat_grad = dot(one_ref[...], ng[...], TN)
    one_grad = dot(ng[pl.ds(0, base), :], feat_two[0], NT) + dot(
        ng[pl.ds(base, base), :], feat_two[1], NT)

    nb = nb_ref[...]
    high = nb // 64
    low = nb - high * 64
    rim_high = dot(high.astype(F32).astype(BF16), chosen)
    rim_low = dot(low.astype(F32).astype(BF16), chosen)
    rim = (rim_high * 64.0 + rim_low).astype(jnp.int32)
    rim_feat = [dot(feat_two[i], chosen).astype(BF16) for i in range(2)]
    for x, y in BESIDE:
        @pl.when(beside(x, y))
        def _():
            halo_copy(-x, -y).wait_recv()
    for o in range(offsets):
        mirror = offsets - 1 - o
        ex, ey = mirror // 9 - 1, mirror // 3 % 3 - 1
        total = jnp.zeros((channels, padded), F32)
        for gx, gy in sorted({(ex, 0), (0, ey), (ex, ey)} - {(0, 0)}):
            b = (gx + 1) * 3 + gy + 1
            index = rim[mirror:mirror + 1, :] - (sites + b * width)
            total = total + dot(halo[b], pick(index, padded))
        ngr[pl.ds(o * channels, channels), :] = total.astype(BF16)
    extra = dot(one_ref[...], ngr[...], TN)
    head = extra.astype(BF16)
    tail = (extra - head.astype(F32)).astype(BF16)
    feat_out_ref[...] = (feat_grad + dot(head, chosen, NT) + dot(tail, chosen, NT)).astype(BF16)
    one_grad = one_grad + dot(ngr[pl.ds(0, base), :], rim_feat[0], NT) + dot(
        ngr[pl.ds(base, base), :], rim_feat[1], NT)
    part[pl.ds(0, base), :] = one_grad.astype(BF16)

    band = n_col * share

    def row_copy(src_row, dst_row, to):
        return remote(part.at[pl.ds(pl.multiple_of(dst_row * band, band), band)], row_in.at[src_row],
                      row_sems.at[0, dst_row], row_sems.at[1, src_row], c, to)

    others(r, n_row, lambda peer: row_copy(r, peer, peer).start())
    row_in[pl.ds(r, 1)] = part[pl.ds(pl.multiple_of(r * band, band), band), :][None]
    others(r, n_row, lambda peer: row_copy(peer, r, r).wait_recv())
    total = row_in[0].astype(F32)
    for i in range(1, n_row):
        total = total + row_in[i].astype(F32)
    mid[...] = total.astype(BF16)

    def col_copy(src_col, dst_col, to):
        return remote(mid.at[pl.ds(pl.multiple_of(dst_col * share, share), share)],
                      col_in.at[src_col], col_sems.at[0, dst_col], col_sems.at[1, src_col], to, r)

    others(c, n_col, lambda peer: col_copy(c, peer, peer).start())
    col_in[pl.ds(c, 1)] = mid[pl.ds(pl.multiple_of(c * share, share), share), :][None]
    others(c, n_col, lambda peer: col_copy(peer, c, c).wait_recv())
    total = col_in[0].astype(F32)
    for i in range(1, n_col):
        total = total + col_in[i].astype(F32)
    fin[...] = total.astype(BF16)

    def gather_col_copy(src_col, dst_col, to):
        return remote(fin, sum_ref.at[r, src_col], gather_col_sems.at[0, dst_col],
                      gather_col_sems.at[1, src_col], to, r)

    others(c, n_col, lambda peer: gather_col_copy(c, peer, peer).start())
    sum_ref[pl.ds(r, 1), pl.ds(c, 1)] = fin[...][None, None]
    others(c, n_col, lambda peer: gather_col_copy(peer, c, c).wait_recv())

    def gather_row_copy(src_row, dst_row, to):
        return remote(sum_ref.at[src_row], sum_ref.at[src_row], gather_row_sems.at[0, dst_row],
                      gather_row_sems.at[1, src_row], c, to)

    others(r, n_row, lambda peer: gather_row_copy(r, peer, peer).start())
    others(r, n_row, lambda peer: gather_row_copy(peer, r, r).wait_recv())

    others(c, n_col, lambda peer: coarse_copy(c, peer, peer).wait_send())
    for x, y in BESIDE:
        @pl.when(beside(x, y))
        def _():
            halo_copy(x, y).wait_send()
    others(r, n_row, lambda peer: row_copy(r, peer, peer).wait_send())
    others(c, n_col, lambda peer: col_copy(c, peer, peer).wait_send())
    others(c, n_col, lambda peer: gather_col_copy(c, peer, peer).wait_send())
    others(r, n_row, lambda peer: gather_row_copy(r, peer, peer).wait_send())


def body(features, preact, coarse_grad, kernel_one, kernel_two, neighbours, send_list,
         parent_slot, child_pos):
    channels, sites = features.shape
    wide, parents = coarse_grad.shape
    offsets = neighbours.shape[0]
    width = send_list.shape[0]
    padded = -(-width // 128) * 128
    n_col, n_row = lax.axis_size("col"), lax.axis_size("row")
    held = parents // n_col
    lines = -(-held // 16) * 16
    pairs = (offsets + 1) // 2
    rows = (pairs + 8) * channels
    share = -(-rows // (n_col * n_row * 16)) * 16
    shape = jax.ShapeDtypeStruct
    coarse = jnp.pad(coarse_grad.T.reshape(n_col, held, wide), ((0, 0), (0, lines - held), (0, 0)))
    two = kernel_two.transpose(0, 2, 1).reshape(8 * channels, wide)
    one = jnp.pad(kernel_one.reshape(offsets * channels, channels), ((0, channels), (0, 0)))
    send = jnp.pad(send_list, (0, padded - width), constant_values=-1)[None, :]
    args = (coarse, parent_slot[None, :], child_pos[None, :], preact, features, two, one, neighbours,
            send)
    vmem = pl.BlockSpec(memory_space=pltpu.VMEM)
    total = n_row * n_col * share
    feat_grad, sums = pl.pallas_call(
        functools.partial(kernel, (n_col, n_row, width, held, share)),
        out_shape=(shape((channels, sites), BF16), shape((n_row, n_col, share, wide), BF16)),
        in_specs=[vmem] * len(args),
        out_specs=(vmem, vmem),
        scratch_shapes=[
            pltpu.VMEM((n_col, lines, wide), BF16),
            pltpu.VMEM((channels, sites), BF16),
            pltpu.VMEM((channels, padded), BF16),
            pltpu.VMEM((9, channels, padded), BF16),
            pltpu.VMEM((2 * pairs * channels, sites), BF16),
            pltpu.VMEM((2 * pairs * channels, padded), BF16),
            pltpu.VMEM((2, 2 * channels, sites), BF16),
            pltpu.VMEM((total, wide), BF16),
            pltpu.VMEM((n_row, n_col * share, wide), BF16),
            pltpu.VMEM((n_col * share, wide), BF16),
            pltpu.VMEM((n_col, share, wide), BF16),
            pltpu.VMEM((share, wide), BF16),
            pltpu.SemaphoreType.DMA((2, n_col)),
            pltpu.SemaphoreType.DMA((2, 9)),
            pltpu.SemaphoreType.DMA((2, n_row)),
            pltpu.SemaphoreType.DMA((2, n_col)),
            pltpu.SemaphoreType.DMA((2, n_col)),
            pltpu.SemaphoreType.DMA((2, n_row)),
        ],
        compiler_params=pltpu.CompilerParams(
            collective_id=0, has_side_effects=True, vmem_limit_bytes=48 * 1024 * 1024),
    )(*args)
    scale = float(sites * n_col * n_row) ** (-0.5)
    sums = sums.reshape(total, wide).astype(F32) * scale
    one_sum = sums[:pairs * channels].reshape(pairs, channels, wide)
    one_sum = jnp.concatenate([one_sum[:, :, :channels], one_sum[:, :, channels:]])[:offsets]
    two_sum = sums[pairs * channels:rows].reshape(8, channels, wide).transpose(0, 2, 1)
    return feat_grad, one_sum, two_sum


def solution(mesh):
    both = ("col", "row")
    placed = (P(None, both), P(None, both), P(None, both), P(), P(), P(None, both), P(both),
              P(both), P(both))
    return jax.shard_map(body, mesh=mesh, in_specs=placed, out_specs=(P(None, both), P(), P()),
                         check_vma=False)
```

time: 425 us -> 52.4 us (0.12)
  local copies, waits for them, and re-layouts: 199 us -> 4.39 us
  waiting for transfers between devices: 136 us -> 0 us
  Pallas kernels: 0 us -> 45.9 us
  matrix products: 42.3 us -> 0 us
  starting transfers between devices: 18.5 us -> 0 us
  between operations: 14.2 us -> 0.77 us
  other arithmetic: 9.83 us -> 1.07 us
    gather x56 -> x0, local copies, waits for them, and re-layouts: 177 us -> none  [the longest x27 86.7 us: per_offset(): near_feat = jnp.take(feat_table, near, axis=1)]
    psum x1 -> x0, waiting for transfers between devices: 131 us -> none  [body(): one_sum, two_sum = lax.psum((one_part, two_part), ('col', 'row'))]
    pallas_call x0 -> x1, Pallas kernels: none -> 45.9 us  [body(): pl.pallas_call(functools.partial(kernel, (n_col, n_row, width, held, shar...]
    dot_general x55 -> x0, matrix products: 41.8 us -> none  [the longest x27 30.3 us: per_offset(): lax.dot_general(weight, near_grad, (((0,), (0,)), ((), ())), preferred_el...]
    dynamic_update_slice x54 -> x0, local copies, waits for them, and re-layouts: 19.1 us -> none  [body(): lax.scan(per_offset, jnp.zeros((channels, sites), jnp.float32), (neighbou...]
    ppermute x4 -> x0, starting transfers between devices: 10.2 us -> none  [the longest x2 7.6 us: extended(): lax.ppermute(lax.slice_in_dim(block, block.shape[dim] - width, None, axis...]
    all_to_all x1 -> x0, starting transfers between devices: 8.31 us -> none  [body(): lax.all_to_all(coarse_grad, 'col', split_axis=1, concat_axis=1, tiled=True)]
  transfers between devices with their start and end apart: 6 -> 0, of which waited for: 3 -> 0; matrix products, arithmetic and copies ran while one was open for 1% -> 0% of each run, Pallas kernels for 0% -> 0%
where the time goes in v1:
time: 52.4 us; the launch traced here: 52.2 us
  Pallas kernels  45.9 us (88%)
  local copies, waits for them, and re-layouts  4.39 us (8%)
  other arithmetic  1.07 us (2%)
  between operations  0.77 us (1%)
    pallas_call x1, Pallas kernels, body(): pl.pallas_call(functools.partial(kernel, (n_col, n_row, width, held, shar...  45.9 us
    unnamed x15, local copies, waits for them, and re-layouts  1.36 us
    pad x1, local copies, waits for them, and re-layouts, body(): jnp.pad(kernel_one.reshape(offsets * channels, channels), ((0, channels),...  1.21 us

profile of v1, /device:TPU:0, one launch (start us, length us, event | category | flops | bytes accessed | tf_op | source)
XLA Modules:
  0.0 52.2 jit_solution(11877474344743115636)
XLA Ops:
  0.6 0.0 copy-start.6
  0.6 0.7 %copy-done.6 = s32[224]{0:T(256)S(1)} copy-done((s32[224]{0:T(256)S(1)}, s32[224]{0:T(256)}, u32[]{:S(2)}) %copy-start.6) | copy-done | bytes 920
  1.3 0.9 %copy.12 = bf16[128,128]{1,0:T(8,128)(2,1)S(1)} copy(bf16[128,128]{0,1:T(8,128)(2,1)} %bitcast.24) | data formatting | bytes 65536 | tf_op jit(solution)/shard_map/transpose | solution.py:239
  2.2 0.0 copy-start
  2.2 0.0 copy-start.1
  2.2 0.0 copy-start.2
  2.2 0.0 copy-start.3
  2.3 0.0 copy-start.4
  2.3 0.0 copy-start.5
  2.3 1.2 %pad.13.one_ref = bf16[1792,64]{1,0:T(8,128)(2,1)S(1)} pad(bf16[1728,64]{1,0:T(8,128)(2,1)} %bitcast.21, bf16[]{:T(256)} %constant.1.clone.1), padding=0_64x0_0 | pad | bytes 450562 | tf_op jit(solution)/shard_map/jit(_pad)/pad | solution.py:241
  3.5 0.0 copy-done
  3.5 0.0 copy-done.1
  3.5 0.0 copy-done.2
  3.5 0.0 copy-done.3
  3.5 0.0 copy-done.4
  3.5 0.0 copy-done.5
  3.5 45.9 %shard_map.112 = (bf16[64,1024]{1,0:T(8,128)(2,1)S(1)}, bf16[2,16,48,128]{3,2,1,0:T(8,128)(2,1)S(1)}) custom-call(bf16[16,16,128]{2,1,0:T(8,128)(2,1)S(1)} %pad.12.coarse_ref, s32[1,1024]{1,0:T(1,128)S(1)} %bitcast.15, s32[1,1024]{1,0:T(1,128)S(1)} %bitcast.16, bf16[64,1024]{1,0:T(8,128)(2,1)S(1)} %copy-done, bf16[64,1024]{1,0:T(8,128)(2,1)S(1)} %copy-done.1, ...), custom_call_target="tpu_custom_call" | custom-call | tf_op jit(solution)/shard_map/pallas_call | solution.py:247
  49.5 0.1 convert_multiply_fusion
  49.6 0.7 %slice.23 = f32[512,128]{1,0:T(8,128)} slice(f32[1536,128]{1,0:T(8,128)S(1)} %bitcast.19), slice={[896:1408], [0:128]} | slice | bytes 524288 | tf_op jit(solution)/shard_map/slice | solution.py:279
  50.3 0.2 fusion
  50.5 1.0 %pad_maximum_fusion = f32[27,64,64]{2,1,0:T(8,128)} fusion(f32[14,64,64]{2,1,0:T(8,128)S(1)} %get-tuple-element.8, f32[14,64,64]{2,1,0:T(8,128)S(1)} %get-tuple-element.7), kind=kLoop, calls=%fused_computation | loop fusion | flops 110592 | bytes 901120 | tf_op jit(solution)/shard_map/concatenate | solution.py:278
  51.5 0.7 %copy.14 = bf16[64,1024]{1,0:T(8,128)(2,1)} copy(bf16[64,1024]{1,0:T(8,128)(2,1)S(1)} %get-tuple-element.12) | data formatting | bytes 262144
  (3 shorter events, 0.1 us)
Async XLA Ops:
  0.6 0.7 %copy-start.6 = (s32[224]{0:T(256)S(1)}, s32[224]{0:T(256)}, u32[]{:S(2)}) copy-start(s32[224]{0:T(256)} %param.15) | copy-start | bytes 2692
  2.2 1.3 %copy-start = (bf16[64,1024]{1,0:T(8,128)(2,1)S(1)}, bf16[64,1024]{1,0:T(8,128)(2,1)}, u32[]{:S(2)}) copy-start(bf16[64,1024]{1,0:T(8,128)(2,1)} %preact_ref.1) | copy-start | bytes 393220
  2.2 1.3 %copy-start.1 = (bf16[64,1024]{1,0:T(8,128)(2,1)S(1)}, bf16[64,1024]{1,0:T(8,128)(2,1)}, u32[]{:S(2)}) copy-start(bf16[64,1024]{1,0:T(8,128)(2,1)} %feat_ref.1) | copy-start | bytes 393220
  2.2 1.3 %copy-start.2 = (bf16[8,128,64]{1,2,0:T(8,128)(2,1)S(1)}, bf16[8,128,64]{1,2,0:T(8,128)(2,1)}, u32[]{:S(2)}) copy-start(bf16[8,128,64]{1,2,0:T(8,128)(2,1)} %param.13) | copy-start | bytes 393220
  2.2 1.3 %copy-start.3 = (s32[27,1024]{1,0:T(8,128)S(1)}, s32[27,1024]{1,0:T(8,128)}, u32[]{:S(2)}) copy-start(s32[27,1024]{1,0:T(8,128)} %nb_ref.1) | copy-start | bytes 331780
  2.3 1.3 %copy-start.4 = (s32[1024]{0:T(1024)S(1)}, s32[1024]{0:T(1024)}, u32[]{:S(2)}) copy-start(s32[1024]{0:T(1024)} %param.16) | copy-start | bytes 12292
  2.3 1.3 %copy-start.5 = (s32[1024]{0:T(1024)S(1)}, s32[1024]{0:T(1024)}, u32[]{:S(2)}) copy-start(s32[1024]{0:T(1024)} %param.17) | copy-start | bytes 12292

commit v2 on v1

v2 whole, which is shorter than its diff:
```python
import functools

import jax
import jax.numpy as jnp
from jax import lax
from jax.experimental import pallas as pl
from jax.experimental.pallas import tpu as pltpu
from jax.sharding import PartitionSpec as P

F32 = jnp.float32
BF16 = jnp.bfloat16
NN = (((1,), (0,)), ((), ()))
NT = (((1,), (1,)), ((), ()))
TN = (((0,), (0,)), ((), ()))
MESH = pl.DeviceIdType.MESH
BESIDE = [(x, y) for x in (-1, 0, 1) for y in (-1, 0, 1) if (x, y) != (0, 0)]


def pick(index_row, rows):
    n = index_row.shape[1]
    spot = lax.broadcasted_iota(jnp.int32, (rows, n), 0)
    return jnp.where(spot == index_row, 1.0, 0.0).astype(BF16)


def dot(a, b, dims=NN):
    return lax.dot_general(a, b, dims, preferred_element_type=F32)


def remote(src, dst, send_sem, recv_sem, col, row):
    return pltpu.make_async_remote_copy(
        src_ref=src, dst_ref=dst, send_sem=send_sem, recv_sem=recv_sem,
        device_id=(col, row), device_id_type=MESH)


def others(me, count, step):
    def one(j, carry):
        step(lax.rem(me + j, count))
        return carry
    lax.fori_loop(1, count, one, 0)


class Sum:
    def __init__(self, place, share, part, row_in, mid, col_in, fin, out, row_sems, col_sems,
                 back_col_sems, back_row_sems):
        self.c, self.r, self.n_col, self.n_row = place
        self.share, self.band = share, share * self.n_col
        self.part, self.row_in, self.mid, self.col_in = part, row_in, mid, col_in
        self.fin, self.out = fin, out
        self.sems = (row_sems, col_sems, back_col_sems, back_row_sems)

    def rows(self, step):
        others(self.r, self.n_row, step)

    def cols(self, step):
        others(self.c, self.n_col, step)

    def row_copy(self, src, dst, to):
        cut = pl.ds(pl.multiple_of(dst * self.band, self.band), self.band)
        return remote(self.part.at[cut], self.row_in.at[src], self.sems[0].at[0, dst],
                      self.sems[0].at[1, src], self.c, to)

    def col_copy(self, src, dst, to):
        cut = pl.ds(pl.multiple_of(dst * self.share, self.share), self.share)
        return remote(self.mid.at[cut], self.col_in.at[src], self.sems[1].at[0, dst],
                      self.sems[1].at[1, src], to, self.r)

    def back_col_copy(self, src, dst, to):
        return remote(self.fin, self.out.at[self.r, src], self.sems[2].at[0, dst],
                      self.sems[2].at[1, src], to, self.r)

    def back_row_copy(self, src, dst, to):
        return remote(self.out.at[src], self.out.at[src], self.sems[3].at[0, dst],
                      self.sems[3].at[1, src], self.c, to)

    def start(self):
        self.rows(lambda peer: self.row_copy(self.r, peer, peer).start())
        self.row_in[pl.ds(self.r, 1)] = self.part[
            pl.ds(pl.multiple_of(self.r * self.band, self.band), self.band), :][None]

    def along_col(self):
        self.rows(lambda peer: self.row_copy(peer, self.r, self.r).wait_recv())
        total = self.row_in[0].astype(F32)
        for i in range(1, self.n_row):
            total = total + self.row_in[i].astype(F32)
        self.mid[...] = total.astype(BF16)
        self.cols(lambda peer: self.col_copy(self.c, peer, peer).start())
        self.col_in[pl.ds(self.c, 1)] = self.mid[
            pl.ds(pl.multiple_of(self.c * self.share, self.share), self.share), :][None]

    def back_col(self):
        self.cols(lambda peer: self.col_copy(peer, self.c, self.c).wait_recv())
        total = self.col_in[0].astype(F32)
        for i in range(1, self.n_col):
            total = total + self.col_in[i].astype(F32)
        self.fin[...] = total.astype(BF16)
        self.cols(lambda peer: self.back_col_copy(self.c, peer, peer).start())
        self.out[pl.ds(self.r, 1), pl.ds(self.c, 1)] = self.fin[...][None, None]

    def back_row(self):
        self.cols(lambda peer: self.back_col_copy(peer, self.c, self.c).wait_recv())
        self.rows(lambda peer: self.back_row_copy(self.r, peer, peer).start())

    def end(self):
        self.rows(lambda peer: self.back_row_copy(peer, self.r, self.r).wait_recv())
        self.rows(lambda peer: self.row_copy(self.r, peer, peer).wait_send())
        self.cols(lambda peer: self.col_copy(self.c, peer, peer).wait_send())
        self.cols(lambda peer: self.back_col_copy(self.c, peer, peer).wait_send())
        self.rows(lambda peer: self.back_row_copy(self.r, peer, peer).wait_send())


def offset_of(x, y, z):
    return (x + 1) * 9 + (y + 1) * 3 + z + 1


def bits(child):
    return child // 4, child // 2 % 2, child % 2


def kernel(sizes, coarse_ref, slot_ref, child_ref, preact_ref, feat_ref, two_ref, one_ref, nb_ref,
           send_ref, feat_out_ref, one_sum_ref, two_sum_ref,
           owners, grad, offer, halo, ng, ngr, feat_two, sort, moves, *rest):
    n_col, n_row, width, held, one_share, two_share = sizes
    channels, sites = feat_ref.shape
    parents = sites // 8
    offsets = nb_ref.shape[0]
    pairs = (offsets + 1) // 2
    padded = send_ref.shape[1]
    c, r = lax.axis_index("col"), lax.axis_index("row")
    place = (c, r, n_col, n_row)
    one_sum = Sum(place, one_share, *rest[0:5], one_sum_ref, *rest[10:14])
    two_sum = Sum(place, two_share, *rest[5:10], two_sum_ref, *rest[14:18])
    coarse_sems, halo_sems = rest[18:]

    def beside(x, y):
        return ((c + x >= 0) & (c + x < n_col) & (r + y >= 0) & (r + y < n_row))

    barrier = pltpu.get_barrier_semaphore()

    def greet(col, row):
        pl.semaphore_signal(barrier, inc=1, device_id=(col, row), device_id_type=MESH)

    others(c, n_col, lambda peer: greet(peer, r))
    others(r, n_row, lambda peer: greet(c, peer))
    count = n_col - 1 + n_row - 1
    for x, y in BESIDE:
        if x != 0 and y != 0:
            there = beside(x, y)

            @pl.when(there)
            def _():
                greet(c + x, r + y)

            count = count + jnp.where(there, 1, 0)
    pl.semaphore_wait(barrier, count)

    def coarse_copy(src_col, dst_col, to):
        return remote(coarse_ref.at[dst_col], owners.at[src_col], coarse_sems.at[0, dst_col],
                      coarse_sems.at[1, src_col], to, r)

    others(c, n_col, lambda peer: coarse_copy(c, peer, peer).start())
    owners[pl.ds(c, 1)] = coarse_ref[pl.ds(c, 1)]
    for x, y in BESIDE:
        @pl.when(jnp.logical_not(beside(x, y)))
        def _():
            halo[(x + 1) * 3 + y + 1] = jnp.zeros(halo.shape[1:], BF16)

    nb = nb_ref[...]
    high = nb // 64
    low = (nb - high * 64).astype(F32).astype(BF16)
    high = high.astype(F32).astype(BF16)

    def entries(onehot, dims=NN):
        return (dot(high, onehot, dims) * 64.0 + dot(low, onehot, dims)).astype(jnp.int32)

    slot = slot_ref[...]
    child = child_ref[...]
    kinds = lax.broadcasted_iota(jnp.int32, (128, sites), 0)
    first = jnp.where((kinds == child) & (slot == 0), 1.0, 0.0).astype(BF16)
    first_nb = entries(first, NT)
    slot_mark = jnp.broadcast_to((slot + 1).astype(F32), (16, sites)).astype(BF16)
    kind = jnp.zeros((16, 128), F32)
    for weight, o in ((4.0, offset_of(-1, 0, 0)), (2.0, offset_of(0, -1, 0)),
                      (1.0, offset_of(0, 0, -1))):
        mark = dot(slot_mark, pick(first_nb[o:o + 1, :], sites))
        kind = kind + jnp.where(mark == 1.0, weight, 0.0)
    corner = dot(kind.astype(BF16), pick(child, 128))[0:1, :].astype(jnp.int32)

    sort[...] = pick(corner * parents + slot, sites)
    feat = dot(feat_ref[...], sort[...], NT).astype(BF16)
    feat_two[0, pl.ds(0, channels), :] = feat
    feat_two[0, pl.ds(channels, channels), :] = jnp.zeros((channels, sites), BF16)
    feat_two[1, pl.ds(0, channels), :] = jnp.zeros((channels, sites), BF16)
    feat_two[1, pl.ds(channels, channels), :] = feat
    sorted_nb = entries(sort[...], NT)
    chosen_slot = pick(slot, parents)
    for o in range(offsets):
        if o != offsets // 2:
            x, y, z = o // 9 - 1, o // 3 % 3 - 1, o % 3 - 1
            at = ((x > 0) * 4 + (y > 0) * 2 + (z > 0)) * parents
            moves[o] = dot(
                chosen_slot, pick(sorted_nb[o:o + 1, at:at + parents], sites)).astype(BF16)
    chosen = pick(send_ref[...], sites)
    rim = entries(chosen)
    rim_feat = dot(feat_ref[...], chosen).astype(BF16)
    blank = jnp.zeros(rim_feat.shape, BF16)

    pre = preact_ref[...].astype(F32)
    gate = jax.nn.sigmoid(pre)
    act = (pre * gate).astype(BF16).astype(F32)
    lines = owners.shape[1]
    chosen_parent = pick(slot // held * lines + slot % held, n_col * lines)
    ng[pl.ds(offsets * channels, channels), :] = jnp.zeros((channels, sites), BF16)
    ngr[pl.ds(offsets * channels, channels), :] = jnp.zeros((channels, padded), BF16)
    others(c, n_col, lambda peer: coarse_copy(peer, c, c).wait_recv())
    all_owned = owners[...].reshape(n_col * lines, owners.shape[2])
    parent = dot(all_owned.astype(F32).T.astype(BF16), chosen_parent).astype(BF16)
    act_grad = jnp.zeros((channels, sites), F32)
    for k in range(8):
        rows = pl.ds(k * channels, channels)
        here = jnp.broadcast_to(child == k, (channels, sites))
        act_grad = jnp.where(here, dot(two_ref[rows, :], parent), act_grad)
    grad[...] = (act_grad * gate * (1.0 + pre * (1.0 - gate))).astype(BF16)
    offer[...] = dot(grad[...], chosen).astype(BF16)

    def halo_copy(x, y):
        b = (x + 1) * 3 + y + 1
        return remote(offer, halo.at[8 - b], halo_sems.at[0, b], halo_sems.at[1, 8 - b],
                      c + x, r + y)

    for x, y in BESIDE:
        @pl.when(beside(x, y))
        def _():
            halo_copy(x, y).start()

    two_rows = 8 * channels
    for k in range(8):
        here = jnp.broadcast_to(child == k, (channels, sites))
        masked = jnp.where(here, act, 0.0).astype(BF16)
        two_sum.part[pl.ds(k * channels, channels), :] = dot(masked, parent, NT).astype(BF16)
    base = pairs * channels
    for piece, used in ((two_sum.part, two_rows), (one_sum.part, base)):
        spare = piece.shape[0] - used
        if spare > 0:
            piece[pl.ds(used, spare), :] = jnp.zeros((spare, piece.shape[1]), BF16)
    two_sum.start()

    near = dot(grad[...], sort[...], NT).astype(BF16)
    blocks = [near[:, k * parents:(k + 1) * parents] for k in range(8)]
    found = {((0, 0, 0), k): blocks[k] for k in range(8)}
    for o in range(offsets):
        if o != offsets // 2:
            step = (o // 9 - 1, o // 3 % 3 - 1, o % 3 - 1)
            ends = [k for k in range(8)
                    if all(s == 0 or b == (s < 0) for s, b in zip(step, bits(k)))]
            moved = dot(jnp.concatenate([blocks[k] for k in ends], axis=0), moves[o]).astype(BF16)
            for i, k in enumerate(ends):
                found[step, k] = moved[i * channels:(i + 1) * channels, :]
    for o in range(offsets):
        move = (1 - o // 9, 1 - o // 3 % 3, 1 - o % 3)
        for k in range(8):
            to = [b + m for b, m in zip(bits(k), move)]
            end = to[0] % 2 * 4 + to[1] % 2 * 2 + to[2] % 2
            ng[pl.ds(o * channels, channels), pl.ds(k * parents, parents)] = (
                found[tuple(t // 2 for t in to), end])
    two_sum.along_col()
    spread = dot(one_ref[...], ng[pl.ds(0, offsets * channels), :], TN)

    def split(values):
        head = values.astype(BF16)
        return head, (values - head.astype(F32)).astype(BF16)

    head, tail = split(spread)
    feat_grad = dot(head, sort[...]) + dot(tail, sort[...])
    one_grad = dot(ng[pl.ds(0, base), :], feat_two[0], NT) + dot(
        ng[pl.ds(base, base), :], feat_two[1], NT)

    for x, y in BESIDE:
        @pl.when(beside(x, y))
        def _():
            halo_copy(-x, -y).wait_recv()
    for o in range(offsets):
        mirror = offsets - 1 - o
        ex, ey = mirror // 9 - 1, mirror // 3 % 3 - 1
        total = jnp.zeros((channels, padded), F32)
        for gx, gy in sorted({(ex, 0), (0, ey), (ex, ey)} - {(0, 0)}):
            b = (gx + 1) * 3 + gy + 1
            index = rim[mirror:mirror + 1, :] - (sites + b * width)
            total = total + dot(halo[b], pick(index, padded))
        ngr[pl.ds(o * channels, channels), :] = total.astype(BF16)
    one_grad = one_grad + dot(
        ngr[pl.ds(0, base), :], jnp.concatenate([rim_feat, blank], axis=0), NT) + dot(
        ngr[pl.ds(base, base), :], jnp.concatenate([blank, rim_feat], axis=0), NT)
    one_sum.part[pl.ds(0, base), :] = one_grad.astype(BF16)
    one_sum.start()
    two_sum.back_col()
    one_sum.along_col()
    head, tail = split(dot(one_ref[...], ngr[pl.ds(0, offsets * channels), :], TN))
    feat_out_ref[...] = (feat_grad + dot(head, chosen, NT) + dot(tail, chosen, NT)).astype(BF16)
    two_sum.back_row()
    one_sum.back_col()
    one_sum.back_row()
    two_sum.end()
    one_sum.end()

    others(c, n_col, lambda peer: coarse_copy(c, peer, peer).wait_send())
    for x, y in BESIDE:
        @pl.when(beside(x, y))
        def _():
            halo_copy(x, y).wait_send()


def body(features, preact, coarse_grad, kernel_one, kernel_two, neighbours, send_list,
         parent_slot, child_pos):
    channels, sites = features.shape
    wide, parents = coarse_grad.shape
    offsets = neighbours.shape[0]
    width = send_list.shape[0]
    padded = -(-width // 128) * 128
    n_col, n_row = lax.axis_size("col"), lax.axis_size("row")
    held = parents // n_col
    lines = -(-held // 16) * 16
    pairs = (offsets + 1) // 2
    one_rows, two_rows = pairs * channels, 8 * channels
    one_share, two_share = (-(-rows // (n_col * n_row * 16)) * 16 for rows in (one_rows, two_rows))
    shape = jax.ShapeDtypeStruct
    coarse = jnp.pad(coarse_grad.T.reshape(n_col, held, wide), ((0, 0), (0, lines - held), (0, 0)))
    two = kernel_two.transpose(0, 2, 1).reshape(8 * channels, wide)
    one = kernel_one.reshape(offsets * channels, channels)
    send = jnp.pad(send_list, (0, padded - width), constant_values=-1)[None, :]
    args = (coarse, parent_slot[None, :], child_pos[None, :], preact, features, two, one, neighbours,
            send)
    vmem = pl.BlockSpec(memory_space=pltpu.VMEM)
    sum_scratch, sum_sems = [], []
    for share in (one_share, two_share):
        sum_scratch += [
            pltpu.VMEM((n_row * n_col * share, wide), BF16),
            pltpu.VMEM((n_row, n_col * share, wide), BF16),
            pltpu.VMEM((n_col * share, wide), BF16),
            pltpu.VMEM((n_col, share, wide), BF16),
            pltpu.VMEM((share, wide), BF16),
        ]
        sum_sems += [pltpu.SemaphoreType.DMA((2, n)) for n in (n_row, n_col, n_col, n_row)]
    feat_grad, one_sum, two_sum = pl.pallas_call(
        functools.partial(kernel, (n_col, n_row, width, held, one_share, two_share)),
        out_shape=(shape((channels, sites), BF16), shape((n_row, n_col, one_share, wide), BF16),
                   shape((n_row, n_col, two_share, wide), BF16)),
        in_specs=[vmem] * len(args),
        out_specs=(vmem, vmem, vmem),
        scratch_shapes=[
            pltpu.VMEM((n_col, lines, wide), BF16),
            pltpu.VMEM((channels, sites), BF16),
            pltpu.VMEM((channels, padded), BF16),
            pltpu.VMEM((9, channels, padded), BF16),
            pltpu.VMEM((2 * pairs * channels, sites), BF16),
            pltpu.VMEM((2 * pairs * channels, padded), BF16),
            pltpu.VMEM((2, 2 * channels, sites), BF16),
            pltpu.VMEM((sites, sites), BF16),
            pltpu.VMEM((offsets, sites // 8, sites // 8), BF16),
            *sum_scratch,
            *sum_sems,
            pltpu.SemaphoreType.DMA((2, n_col)),
            pltpu.SemaphoreType.DMA((2, 9)),
        ],
        compiler_params=pltpu.CompilerParams(
            collective_id=0, has_side_effects=True, vmem_limit_bytes=48 * 1024 * 1024),
    )(*args)
    scale = float(sites * n_col * n_row) ** (-0.5)
    one_sum = one_sum.reshape(-1, wide)[:one_rows].reshape(pairs, channels, wide)
    one_sum = jnp.concatenate([one_sum[:, :, :channels], one_sum[:, :, channels:]])[:offsets]
    two_sum = two_sum.reshape(-1, wide)[:two_rows].reshape(8, channels, wide).transpose(0, 2, 1)
    return feat_grad, one_sum.astype(F32) * scale, two_sum.astype(F32) * scale


def solution(mesh):
    both = ("col", "row")
    placed = (P(None, both), P(None, both), P(None, both), P(), P(), P(None, both), P(both),
              P(both), P(both))
    return jax.shard_map(body, mesh=mesh, in_specs=placed, out_specs=(P(None, both), P(), P()),
                         check_vma=False)
```

time: 52.4 us -> 46 us (0.88)
  Pallas kernels: 45.9 us -> 36.2 us
  local copies, waits for them, and re-layouts: 4.39 us -> 6.8 us
  other arithmetic: 1.07 us -> 1.75 us
    pallas_call x1, Pallas kernels: 45.9 us -> 36.2 us  [body(): pl.pallas_call(functools.partial(kernel, (n_col, n_row, width, held, one_...]
    unnamed x15 -> x17, local copies, waits for them, and re-layouts: 1.36 us -> 5.74 us
    mul x1 -> x2, other arithmetic: 0.06 us -> 1.75 us  [body(): return (feat_grad, one_sum.astype(F32) * scale, two_sum.astype(F32) * scale)]
    pad x1 -> x0, local copies, waits for them, and re-layouts: 1.21 us -> none  [body(): jnp.pad(kernel_one.reshape(offsets * channels, channels), ((0, channels),...]
    concatenate x1 -> x0, other arithmetic: 1.01 us -> none  [body(): jnp.concatenate([one_sum[:, :, :channels], one_sum[:, :, channels:]])]
    slice x2 -> x1, local copies, waits for them, and re-layouts: 0.75 us -> 0.02 us  [body(): one_sum.reshape(-1, wide)[:one_rows].reshape(pairs, channels, wide)]
where the time goes in v2:
time: 46 us; the launch traced here: 45.5 us
  Pallas kernels  36.2 us (79%)
  local copies, waits for them, and re-layouts  6.8 us (15%)
  other arithmetic  1.75 us (4%)
  between operations  0.69 us (2%)
    pallas_call x1, Pallas kernels, body(): pl.pallas_call(functools.partial(kernel, (n_col, n_row, width, held, one_...  36.2 us
    unnamed x17, local copies, waits for them, and re-layouts  5.74 us
    mul x2, other arithmetic, body(): return (feat_grad, one_sum.astype(F32) * scale, two_sum.astype(F32) * scale)  1.75 us

profile of v2, /device:TPU:0, one launch (start us, length us, event | category | flops | bytes accessed | tf_op | source)
XLA Modules:
  0.0 45.5 jit_solution(14087435555502448290)
XLA Ops:
  0.6 0.0 copy-start.1
  0.6 0.9 %copy.12 = bf16[128,128]{1,0:T(8,128)(2,1)S(1)} copy(bf16[128,128]{0,1:T(8,128)(2,1)} %bitcast.23) | data formatting | bytes 65536 | tf_op jit(solution)/shard_map/transpose | solution.py:326
  1.5 0.0 copy-start.7
  1.6 0.7 %copy-done.7 = s32[224]{0:T(256)S(1)} copy-done((s32[224]{0:T(256)S(1)}, s32[224]{0:T(256)}, u32[]{:S(2)}) %copy-start.7) | copy-done | bytes 920
  2.2 0.0 copy-start.6
  2.2 0.0 copy-start.5
  2.2 0.0 copy-done.1
  2.2 0.7 %copy-done.6 = s32[1024]{0:T(1024)S(1)} copy-done((s32[1024]{0:T(1024)S(1)}, s32[1024]{0:T(1024)}, u32[]{:S(2)}) %copy-start.6) | copy-done | bytes 4120
  2.9 0.0 copy-done.5
  2.9 0.0 copy-start
  2.9 1.0 %copy-done = bf16[27,64,64]{2,1,0:T(8,128)(2,1)S(1)} copy-done((bf16[27,64,64]{2,1,0:T(8,128)(2,1)S(1)}, bf16[27,64,64]{2,1,0:T(8,128)(2,1)}, u32[]{:S(2)}) %copy-start) | copy-done | bytes 221208
  4.0 0.0 copy-start.2
  4.0 0.9 %copy-done.2 = bf16[64,1024]{1,0:T(8,128)(2,1)S(1)} copy-done((bf16[64,1024]{1,0:T(8,128)(2,1)S(1)}, bf16[64,1024]{1,0:T(8,128)(2,1)}, u32[]{:S(2)}) %copy-start.2) | copy-done | bytes 131096
  4.9 0.0 copy-start.3
  4.9 0.9 %copy-done.3 = bf16[8,128,64]{1,2,0:T(8,128)(2,1)S(1)} copy-done((bf16[8,128,64]{1,2,0:T(8,128)(2,1)S(1)}, bf16[8,128,64]{1,2,0:T(8,128)(2,1)}, u32[]{:S(2)}) %copy-start.3) | copy-done | bytes 131096
  5.8 0.0 copy-start.4
  5.8 0.9 %copy-done.4 = s32[27,1024]{1,0:T(8,128)S(1)} copy-done((s32[27,1024]{1,0:T(8,128)S(1)}, s32[27,1024]{1,0:T(8,128)}, u32[]{:S(2)}) %copy-start.4) | copy-done | bytes 110616
  6.7 36.2 %shard_map.112 = (bf16[64,1024]{1,0:T(8,128)(2,1)S(1)}, bf16[2,16,32,128]{3,2,1,0:T(8,128)(2,1)S(1)}, bf16[2,16,16,128]{3,2,1,0:T(8,128)(2,1)S(1)}) custom-call(bf16[16,16,128]{2,1,0:T(8,128)(2,1)S(1)} %pad.8.coarse_ref, s32[1,1024]{1,0:T(1,128)S(1)} %bitcast.17, s32[1,1024]{1,0:T(1,128)S(1)} %bitcast.18, bf16[64,1024]{1,0:T(8,128)(2,1)S(1)} %copy-done.1, ...), custom_call_target="tpu_custom_call" | custom-call | tf_op jit(solution)/shard_map/pallas_call | solution.py:343
  42.9 0.1 fusion
  43.0 1.0 %convert_multiply_fusion = f32[27,64,64]{2,1,0:T(8,128)} fusion(bf16[14,64,64]{2,1,0:T(8,128)(2,1)S(1)} %get-tuple-element.10, bf16[14,64,64]{2,1,0:T(8,128)(2,1)S(1)} %get-tuple-element.9), kind=kLoop, calls=%fused_computation | loop fusion | flops 331776 | bytes 671744 | tf_op jit(solution)/shard_map/mul | solution.py:371
  44.1 0.7 %convert_multiply_fusion.1 = f32[2,16,16,128]{3,2,1,0:T(8,128)} fusion(bf16[2,16,16,128]{3,2,1,0:T(8,128)(2,1)S(1)} %get-tuple-element.8), kind=kLoop, calls=%fused_computation.2 | loop fusion | flops 131072 | bytes 393216 | tf_op jit(solution)/shard_map/mul | solution.py:371
  44.8 0.7 %copy.14 = bf16[64,1024]{1,0:T(8,128)(2,1)} copy(bf16[64,1024]{1,0:T(8,128)(2,1)S(1)} %get-tuple-element.14) | data formatting | bytes 262144
  (3 shorter events, 0.0 us)
Async XLA Ops:
  0.6 1.6 %copy-start.1 = (bf16[64,1024]{1,0:T(8,128)(2,1)S(1)}, bf16[64,1024]{1,0:T(8,128)(2,1)}, u32[]{:S(2)}) copy-start(bf16[64,1024]{1,0:T(8,128)(2,1)} %preact_ref.1) | copy-start | bytes 393220
  1.5 0.7 %copy-start.7 = (s32[224]{0:T(256)S(1)}, s32[224]{0:T(256)}, u32[]{:S(2)}) copy-start(s32[224]{0:T(256)} %param.15) | copy-start | bytes 2692
  2.2 0.7 %copy-start.6 = (s32[1024]{0:T(1024)S(1)}, s32[1024]{0:T(1024)}, u32[]{:S(2)}) copy-start(s32[1024]{0:T(1024)} %param.17) | copy-start | bytes 12292
  2.2 0.7 %copy-start.5 = (s32[1024]{0:T(1024)S(1)}, s32[1024]{0:T(1024)}, u32[]{:S(2)}) copy-start(s32[1024]{0:T(1024)} %param.16) | copy-start | bytes 12292
  2.9 1.0 %copy-start = (bf16[27,64,64]{2,1,0:T(8,128)(2,1)S(1)}, bf16[27,64,64]{2,1,0:T(8,128)(2,1)}, u32[]{:S(2)}) copy-start(bf16[27,64,64]{2,1,0:T(8,128)(2,1)} %param.12) | copy-start | bytes 663556
  4.0 0.9 %copy-start.2 = (bf16[64,1024]{1,0:T(8,128)(2,1)S(1)}, bf16[64,1024]{1,0:T(8,128)(2,1)}, u32[]{:S(2)}) copy-start(bf16[64,1024]{1,0:T(8,128)(2,1)} %feat_ref.1) | copy-start | bytes 393220
  4.9 0.9 %copy-start.3 = (bf16[8,128,64]{1,2,0:T(8,128)(2,1)S(1)}, bf16[8,128,64]{1,2,0:T(8,128)(2,1)}, u32[]{:S(2)}) copy-start(bf16[8,128,64]{1,2,0:T(8,128)(2,1)} %param.13) | copy-start | bytes 393220
  5.8 0.9 %copy-start.4 = (s32[27,1024]{1,0:T(8,128)S(1)}, s32[27,1024]{1,0:T(8,128)}, u32[]{:S(2)}) copy-start(s32[27,1024]{1,0:T(8,128)} %nb_ref.1) | copy-start | bytes 331780

commit v3 on v2

--- a/solution.py
+++ b/solution.py
@@ -33,10 +33,12 @@
 
 
 def others(me, count, step):
-    def one(j, carry):
+    for j in range(1, count):
         step(lax.rem(me + j, count))
-        return carry
-    lax.fori_loop(1, count, one, 0)
+
+
+def landed(pieces, sem):
+    pltpu.make_async_copy(pieces, pieces, sem).wait()
 
 
 class Sum:
@@ -56,21 +58,21 @@
 
     def row_copy(self, src, dst, to):
         cut = pl.ds(pl.multiple_of(dst * self.band, self.band), self.band)
-        return remote(self.part.at[cut], self.row_in.at[src], self.sems[0].at[0, dst],
-                      self.sems[0].at[1, src], self.c, to)
+        return remote(self.part.at[cut], self.row_in.at[src], self.sems[0].at[0],
+                      self.sems[0].at[1], self.c, to)
 
     def col_copy(self, src, dst, to):
         cut = pl.ds(pl.multiple_of(dst * self.share, self.share), self.share)
-        return remote(self.mid.at[cut], self.col_in.at[src], self.sems[1].at[0, dst],
-                      self.sems[1].at[1, src], to, self.r)
+        return remote(self.mid.at[cut], self.col_in.at[src], self.sems[1].at[0],
+                      self.sems[1].at[1], to, self.r)
 
     def back_col_copy(self, src, dst, to):
-        return remote(self.fin, self.out.at[self.r, src], self.sems[2].at[0, dst],
-                      self.sems[2].at[1, src], to, self.r)
+        return remote(self.fin, self.out.at[self.r, src], self.sems[2].at[0],
+                      self.sems[2].at[1], to, self.r)
 
     def back_row_copy(self, src, dst, to):
-        return remote(self.out.at[src], self.out.at[src], self.sems[3].at[0, dst],
-                      self.sems[3].at[1, src], self.c, to)
+        return remote(self.out.at[src], self.out.at[src], self.sems[3].at[0],
+                      self.sems[3].at[1], self.c, to)
 
     def start(self):
         self.rows(lambda peer: self.row_copy(self.r, peer, peer).start())
@@ -78,7 +80,7 @@
             pl.ds(pl.multiple_of(self.r * self.band, self.band), self.band), :][None]
 
     def along_col(self):
-        self.rows(lambda peer: self.row_copy(peer, self.r, self.r).wait_recv())
+        landed(self.row_in.at[pl.ds(0, self.n_row - 1)], self.sems[0].at[1])
         total = self.row_in[0].astype(F32)
         for i in range(1, self.n_row):
             total = total + self.row_in[i].astype(F32)
@@ -88,7 +90,7 @@
             pl.ds(pl.multiple_of(self.c * self.share, self.share), self.share), :][None]
 
     def back_col(self):
-        self.cols(lambda peer: self.col_copy(peer, self.c, self.c).wait_recv())
+        landed(self.col_in.at[pl.ds(0, self.n_col - 1)], self.sems[1].at[1])
         total = self.col_in[0].astype(F32)
         for i in range(1, self.n_col):
             total = total + self.col_in[i].astype(F32)
@@ -97,15 +99,15 @@
         self.out[pl.ds(self.r, 1), pl.ds(self.c, 1)] = self.fin[...][None, None]
 
     def back_row(self):
-        self.cols(lambda peer: self.back_col_copy(peer, self.c, self.c).wait_recv())
+        landed(self.out.at[0, pl.ds(0, self.n_col - 1)], self.sems[2].at[1])
         self.rows(lambda peer: self.back_row_copy(self.r, peer, peer).start())
 
     def end(self):
-        self.rows(lambda peer: self.back_row_copy(peer, self.r, self.r).wait_recv())
-        self.rows(lambda peer: self.row_copy(self.r, peer, peer).wait_send())
-        self.cols(lambda peer: self.col_copy(self.c, peer, peer).wait_send())
-        self.cols(lambda peer: self.back_col_copy(self.c, peer, peer).wait_send())
-        self.rows(lambda peer: self.back_row_copy(self.r, peer, peer).wait_send())
+        landed(self.out.at[pl.ds(0, self.n_row - 1)], self.sems[3].at[1])
+        landed(self.row_in.at[pl.ds(0, self.n_row - 1)], self.sems[0].at[0])
+        landed(self.col_in.at[pl.ds(0, self.n_col - 1)], self.sems[1].at[0])
+        landed(self.col_in.at[pl.ds(0, self.n_col - 1)], self.sems[2].at[0])
+        landed(self.out.at[pl.ds(0, self.n_row - 1)], self.sems[3].at[0])
 
 
 def offset_of(x, y, z):
@@ -116,9 +118,19 @@
     return child // 4, child // 2 % 2, child % 2
 
 
-def kernel(sizes, coarse_ref, slot_ref, child_ref, preact_ref, feat_ref, two_ref, one_ref, nb_ref,
-           send_ref, feat_out_ref, one_sum_ref, two_sum_ref,
-           owners, grad, offer, halo, ng, ngr, feat_two, sort, moves, *rest):
+def kernel(sizes, coarse_ref, *refs):
+    count = 8
+    load_sems = refs[-count - 1]
+    held = refs[-count:]
+    loads = [pltpu.make_async_copy(refs[i], held[i], load_sems.at[i]) for i in range(count)]
+    for load in loads:
+        load.start()
+    work(sizes, loads, load_sems.at[count], coarse_ref, *held, *refs[count:-count - 1])
+
+
+def work(sizes, loads, own_sem, coarse_ref, slot_ref, child_ref, send_ref, nb_ref, feat_ref, preact_ref,
+         two_ref, one_ref, feat_out_ref, one_sum_ref, two_sum_ref,
+         owners, grad, offer, halo, ng, ngr, feat_two, sort, moves, *rest):
     n_col, n_row, width, held, one_share, two_share = sizes
     channels, sites = feat_ref.shape
     parents = sites // 8
@@ -154,29 +166,39 @@
     pl.semaphore_wait(barrier, count)
 
     def coarse_copy(src_col, dst_col, to):
-        return remote(coarse_ref.at[dst_col], owners.at[src_col], coarse_sems.at[0, dst_col],
-                      coarse_sems.at[1, src_col], to, r)
+        return remote(coarse_ref.at[dst_col], owners.at[src_col], coarse_sems.at[0],
+                      coarse_sems.at[1], to, r)
 
     others(c, n_col, lambda peer: coarse_copy(c, peer, peer).start())
-    owners[pl.ds(c, 1)] = coarse_ref[pl.ds(c, 1)]
+    own = pltpu.make_async_copy(coarse_ref.at[c], owners.at[c], own_sem)
+    own.start()
     for x, y in BESIDE:
         @pl.when(jnp.logical_not(beside(x, y)))
         def _():
             halo[(x + 1) * 3 + y + 1] = jnp.zeros(halo.shape[1:], BF16)
 
+    for load in loads[:5]:
+        load.wait()
+
     nb = nb_ref[...]
     high = nb // 64
     low = (nb - high * 64).astype(F32).astype(BF16)
     high = high.astype(F32).astype(BF16)
 
+    pad = jnp.zeros((-offsets % 16, sites), BF16)
+    table = jnp.concatenate([high, pad, low, pad, feat_ref[...]], axis=0)
+    low_at = offsets + pad.shape[0]
+
     def entries(onehot, dims=NN):
-        return (dot(high, onehot, dims) * 64.0 + dot(low, onehot, dims)).astype(jnp.int32)
+        got = dot(table, onehot, dims)
+        entry = got[:offsets] * 64.0 + got[low_at:low_at + offsets]
+        return entry.astype(jnp.int32), got[2 * low_at:].astype(BF16)
 
     slot = slot_ref[...]
     child = child_ref[...]
     kinds = lax.broadcasted_iota(jnp.int32, (128, sites), 0)
     first = jnp.where((kinds == child) & (slot == 0), 1.0, 0.0).astype(BF16)
-    first_nb = entries(first, NT)
+    first_nb, _ = entries(first, NT)
     slot_mark = jnp.broadcast_to((slot + 1).astype(F32), (16, sites)).astype(BF16)
     kind = jnp.zeros((16, 128), F32)
     for weight, o in ((4.0, offset_of(-1, 0, 0)), (2.0, offset_of(0, -1, 0)),
@@ -186,24 +208,28 @@
     corner = dot(kind.astype(BF16), pick(child, 128))[0:1, :].astype(jnp.int32)
 
     sort[...] = pick(corner * parents + slot, sites)
-    feat = dot(feat_ref[...], sort[...], NT).astype(BF16)
+    sorted_nb, feat = entries(sort[...], NT)
     feat_two[0, pl.ds(0, channels), :] = feat
     feat_two[0, pl.ds(channels, channels), :] = jnp.zeros((channels, sites), BF16)
     feat_two[1, pl.ds(0, channels), :] = jnp.zeros((channels, sites), BF16)
     feat_two[1, pl.ds(channels, channels), :] = feat
-    sorted_nb = entries(sort[...], NT)
     chosen_slot = pick(slot, parents)
-    for o in range(offsets):
-        if o != offsets // 2:
-            x, y, z = o // 9 - 1, o // 3 % 3 - 1, o % 3 - 1
-            at = ((x > 0) * 4 + (y > 0) * 2 + (z > 0)) * parents
-            moves[o] = dot(
-                chosen_slot, pick(sorted_nb[o:o + 1, at:at + parents], sites)).astype(BF16)
+    def ahead(o):
+        x, y, z = o // 9 - 1, o // 3 % 3 - 1, o % 3 - 1
+        at = ((x > 0) * 4 + (y > 0) * 2 + (z > 0)) * parents
+        return sorted_nb[o:o + 1, at:at + parents]
+
+    for o in range(offsets // 2):
+        mirror = offsets - 1 - o
+        both = jnp.concatenate([ahead(o), ahead(mirror)], axis=1)
+        found = dot(chosen_slot, pick(both, sites)).astype(BF16)
+        moves[o] = found[:, :parents]
+        moves[mirror] = found[:, parents:]
     chosen = pick(send_ref[...], sites)
-    rim = entries(chosen)
-    rim_feat = dot(feat_ref[...], chosen).astype(BF16)
+    rim, rim_feat = entries(chosen)
     blank = jnp.zeros(rim_feat.shape, BF16)
 
+    loads[5].wait()
     pre = preact_ref[...].astype(F32)
     gate = jax.nn.sigmoid(pre)
     act = (pre * gate).astype(BF16).astype(F32)
@@ -211,14 +237,16 @@
     chosen_parent = pick(slot // held * lines + slot % held, n_col * lines)
     ng[pl.ds(offsets * channels, channels), :] = jnp.zeros((channels, sites), BF16)
     ngr[pl.ds(offsets * channels, channels), :] = jnp.zeros((channels, padded), BF16)
-    others(c, n_col, lambda peer: coarse_copy(peer, c, c).wait_recv())
+    own.wait()
+    landed(owners.at[pl.ds(0, n_col - 1)], coarse_sems.at[1])
     all_owned = owners[...].reshape(n_col * lines, owners.shape[2])
     parent = dot(all_owned.astype(F32).T.astype(BF16), chosen_parent).astype(BF16)
-    act_grad = jnp.zeros((channels, sites), F32)
-    for k in range(8):
-        rows = pl.ds(k * channels, channels)
+    loads[6].wait()
+    products = dot(two_ref[...], parent)
+    act_grad = products[:channels]
+    for k in range(1, 8):
         here = jnp.broadcast_to(child == k, (channels, sites))
-        act_grad = jnp.where(here, dot(two_ref[rows, :], parent), act_grad)
+        act_grad = jnp.where(here, products[k * channels:(k + 1) * channels], act_grad)
     grad[...] = (act_grad * gate * (1.0 + pre * (1.0 - gate))).astype(BF16)
     offer[...] = dot(grad[...], chosen).astype(BF16)
 
@@ -233,10 +261,10 @@
             halo_copy(x, y).start()
 
     two_rows = 8 * channels
-    for k in range(8):
-        here = jnp.broadcast_to(child == k, (channels, sites))
-        masked = jnp.where(here, act, 0.0).astype(BF16)
-        two_sum.part[pl.ds(k * channels, channels), :] = dot(masked, parent, NT).astype(BF16)
+    masked = jnp.concatenate([
+        jnp.where(jnp.broadcast_to(child == k, (channels, sites)), act, 0.0).astype(BF16)
+        for k in range(8)], axis=0)
+    two_sum.part[pl.ds(0, two_rows), :] = dot(masked, parent, NT).astype(BF16)
     base = pairs * channels
     for piece, used in ((two_sum.part, two_rows), (one_sum.part, base)):
         spare = piece.shape[0] - used
@@ -263,14 +291,17 @@
             ng[pl.ds(o * channels, channels), pl.ds(k * parents, parents)] = (
                 found[tuple(t // 2 for t in to), end])
     two_sum.along_col()
+    loads[7].wait()
     spread = dot(one_ref[...], ng[pl.ds(0, offsets * channels), :], TN)
 
     def split(values):
         head = values.astype(BF16)
-        return head, (values - head.astype(F32)).astype(BF16)
-
-    head, tail = split(spread)
-    feat_grad = dot(head, sort[...]) + dot(tail, sort[...])
+        return jnp.concatenate([head, (values - head.astype(F32)).astype(BF16)], axis=0)
+
+    def joined(halves):
+        return halves[:channels] + halves[channels:]
+
+    feat_grad = joined(dot(split(spread), sort[...]))
     one_grad = dot(ng[pl.ds(0, base), :], feat_two[0], NT) + dot(
         ng[pl.ds(base, base), :], feat_two[1], NT)
 
@@ -294,19 +325,44 @@
     one_sum.start()
     two_sum.back_col()
     one_sum.along_col()
-    head, tail = split(dot(one_ref[...], ngr[pl.ds(0, offsets * channels), :], TN))
-    feat_out_ref[...] = (feat_grad + dot(head, chosen, NT) + dot(tail, chosen, NT)).astype(BF16)
+    extra = dot(one_ref[...], ngr[pl.ds(0, offsets * channels), :], TN)
+    feat_out_ref[...] = (feat_grad + joined(dot(split(extra), chosen, NT))).astype(BF16)
     two_sum.back_row()
     one_sum.back_col()
     one_sum.back_row()
     two_sum.end()
     one_sum.end()
 
-    others(c, n_col, lambda peer: coarse_copy(c, peer, peer).wait_send())
+    landed(owners.at[pl.ds(0, n_col - 1)], coarse_sems.at[0])
     for x, y in BESIDE:
         @pl.when(beside(x, y))
         def _():
             halo_copy(x, y).wait_send()
+
+
+def finish(scale, feat_in, one_in, two_in, feat_out, one_out, two_out, feat_ref, one_ref, two_ref,
+           one, two, sems):
+    loads = [pltpu.make_async_copy(src, dst, sems.at[3 + i]) for i, (src, dst) in enumerate(
+        ((feat_in, feat_ref), (one_in, one_ref), (two_in, two_ref)))]
+    for load in loads:
+        load.start()
+    offsets, channels, _ = one.shape
+    pairs = (offsets + 1) // 2
+    sent = [pltpu.make_async_copy(src, dst, sems.at[i])
+            for i, (src, dst) in enumerate(((feat_ref, feat_out), (one, one_out), (two, two_out)))]
+    loads[0].wait()
+    sent[0].start()
+    loads[1].wait()
+    sums = one_ref[pl.ds(0, pairs * channels), :].astype(F32) * scale
+    sums = sums.reshape(pairs, channels, 2 * channels)
+    one[pl.ds(0, pairs)] = sums[:, :, :channels]
+    one[pl.ds(pairs, offsets - pairs)] = sums[:offsets - pairs, :, channels:]
+    sent[1].start()
+    loads[2].wait()
+    two[...] = two_ref[pl.ds(0, two.shape[0]), :].astype(F32) * scale
+    sent[2].start()
+    for copy in sent:
+        copy.wait()
 
 
 def body(features, preact, coarse_grad, kernel_one, kernel_two, neighbours, send_list,
@@ -327,8 +383,8 @@
     two = kernel_two.transpose(0, 2, 1).reshape(8 * channels, wide)
     one = kernel_one.reshape(offsets * channels, channels)
     send = jnp.pad(send_list, (0, padded - width), constant_values=-1)[None, :]
-    args = (coarse, parent_slot[None, :], child_pos[None, :], preact, features, two, one, neighbours,
-            send)
+    held_args = (parent_slot[None, :], child_pos[None, :], send, neighbours, features, preact, two, one)
+    anywhere = pl.BlockSpec(memory_space=pl.ANY)
     vmem = pl.BlockSpec(memory_space=pltpu.VMEM)
     sum_scratch, sum_sems = [], []
     for share in (one_share, two_share):
@@ -339,12 +395,12 @@
             pltpu.VMEM((n_col, share, wide), BF16),
             pltpu.VMEM((share, wide), BF16),
         ]
-        sum_sems += [pltpu.SemaphoreType.DMA((2, n)) for n in (n_row, n_col, n_col, n_row)]
+        sum_sems += [pltpu.SemaphoreType.DMA((2,))] * 4
     feat_grad, one_sum, two_sum = pl.pallas_call(
         functools.partial(kernel, (n_col, n_row, width, held, one_share, two_share)),
         out_shape=(shape((channels, sites), BF16), shape((n_row, n_col, one_share, wide), BF16),
                    shape((n_row, n_col, two_share, wide), BF16)),
-        in_specs=[vmem] * len(args),
+        in_specs=[anywhere] * (1 + len(held_args)),
         out_specs=(vmem, vmem, vmem),
         scratch_shapes=[
             pltpu.VMEM((n_col, lines, wide), BF16),
@@ -358,17 +414,29 @@
             pltpu.VMEM((offsets, sites // 8, sites // 8), BF16),
             *sum_scratch,
             *sum_sems,
-            pltpu.SemaphoreType.DMA((2, n_col)),
+            pltpu.SemaphoreType.DMA((2,)),
             pltpu.SemaphoreType.DMA((2, 9)),
+            pltpu.SemaphoreType.DMA((1 + len(held_args),)),
+            *[pltpu.VMEM(x.shape, x.dtype) for x in held_args],
         ],
         compiler_params=pltpu.CompilerParams(
-            collective_id=0, has_side_effects=True, vmem_limit_bytes=48 * 1024 * 1024),
-    )(*args)
+            collective_id=0, has_side_effects=True, vmem_limit_bytes=56 * 1024 * 1024),
+    )(coarse, *held_args)
     scale = float(sites * n_col * n_row) ** (-0.5)
-    one_sum = one_sum.reshape(-1, wide)[:one_rows].reshape(pairs, channels, wide)
-    one_sum = jnp.concatenate([one_sum[:, :, :channels], one_sum[:, :, channels:]])[:offsets]
-    two_sum = two_sum.reshape(-1, wide)[:two_rows].reshape(8, channels, wide).transpose(0, 2, 1)
-    return feat_grad, one_sum.astype(F32) * scale, two_sum.astype(F32) * scale
+    sums = feat_grad, one_sum.reshape(-1, wide), two_sum.reshape(-1, wide)
+    outs = (feat_grad.shape, BF16), ((offsets, channels, channels), F32), ((two_rows, wide), F32)
+    feat_grad, one_sum, two_sum = pl.pallas_call(
+        functools.partial(finish, scale),
+        out_shape=tuple(shape(*out) for out in outs),
+        in_specs=[anywhere] * 3,
+        out_specs=(anywhere,) * 3,
+        scratch_shapes=[
+            *[pltpu.VMEM(x.shape, BF16) for x in sums],
+            pltpu.VMEM(*outs[1]), pltpu.VMEM(*outs[2]), pltpu.SemaphoreType.DMA((6,)),
+        ],
+        compiler_params=pltpu.CompilerParams(vmem_limit_bytes=56 * 1024 * 1024),
+    )(*sums)
+    return feat_grad, one_sum, two_sum.reshape(8, channels, wide).transpose(0, 2, 1)
 
 
 def solution(mesh):

time: 46 us -> 38.6 us (0.84)
  local copies, waits for them, and re-layouts: 6.8 us -> 2.75 us
  other arithmetic: 1.75 us -> 0 us
  Pallas kernels: 36.2 us -> 35 us
    unnamed x17 -> x2, local copies, waits for them, and re-layouts: 5.74 us -> 0.67 us
    pallas_call x1, Pallas kernels: 36.2 us -> 32.8 us  [body(): pl.pallas_call(functools.partial(kernel, (n_col, n_row, width, held, one_...]
    pallas_call x0 -> x1, Pallas kernels: none -> 2.25 us  [body(): pl.pallas_call(functools.partial(finish, scale), out_shape=tuple((shape(*...]
    mul x2 -> x0, other arithmetic: 1.75 us -> none  [body(): return (feat_grad, one_sum.astype(F32) * scale, two_sum.astype(F32) * scale)]
    pad x1, local copies, waits for them, and re-layouts: 0.01 us -> 0.65 us  [body(): jnp.pad(coarse_grad.T.reshape(n_col, held, wide), ((0, 0), (0, lines - he...]
    pad x1, local copies, waits for them, and re-layouts: 0.01 us -> 0.56 us  [body(): send = jnp.pad(send_list, (0, padded - width), constant_values=-1)[None, :]]
where the time goes in v3:
time: 38.6 us; the launch traced here: 38.4 us
  Pallas kernels  35 us (91%)
  local copies, waits for them, and re-layouts  2.75 us (7%)
  between operations  0.65 us (2%)
    pallas_call x1, Pallas kernels, body(): pl.pallas_call(functools.partial(kernel, (n_col, n_row, width, held, one_...  32.8 us
    pallas_call x1, Pallas kernels, body(): pl.pallas_call(functools.partial(finish, scale), out_shape=tuple((shape(*...  2.25 us
    transpose x1, local copies, waits for them, and re-layouts, body(): coarse_grad.T.reshape(n_col, held, wide)  0.86 us

profile of v3, /device:TPU:0, one launch (start us, length us, event | category | flops | bytes accessed | tf_op | source)
XLA Modules:
  0.0 38.4 jit_solution(3195120629187427671)
XLA Ops:
  0.6 0.0 copy-start
  0.6 0.7 %copy-done = s32[224]{0:T(256)S(1)} copy-done((s32[224]{0:T(256)S(1)}, s32[224]{0:T(256)}, u32[]{:S(2)}) %copy-start) | copy-done | bytes 920
  1.3 0.6 %pad.9 = s32[256]{0:T(256)} pad(s32[224]{0:T(256)S(1)} %copy-done, s32[]{:T(128)} %constant.4.clone.1), padding=0_32 | pad | bytes 1924 | tf_op jit(solution)/shard_map/jit(_pad)/pad | solution.py:385
  1.9 0.9 %copy.12 = bf16[128,128]{1,0:T(8,128)(2,1)S(1)} copy(bf16[128,128]{0,1:T(8,128)(2,1)} %bitcast.19) | data formatting | bytes 65536 | tf_op jit(solution)/shard_map/transpose | solution.py:382
  2.7 0.7 %pad.8.coarse_ref = bf16[16,16,128]{2,1,0:T(8,128)(2,1)} pad(bf16[16,8,128]{2,1,0:T(8,128)(2,1)S(1)} %bitcast.17, bf16[]{:T(256)} %constant.1.clone.1), padding=0_0x0_8x0_0 | pad | bytes 98306 | tf_op jit(solution)/shard_map/jit(_pad)/pad | solution.py:382
  3.4 32.8 %shard_map.112 = (bf16[64,1024]{1,0:T(8,128)(2,1)}, bf16[2,16,32,128]{3,2,1,0:T(8,128)(2,1)}, bf16[2,16,16,128]{3,2,1,0:T(8,128)(2,1)}) custom-call(bf16[16,16,128]{2,1,0:T(8,128)(2,1)} %pad.8.coarse_ref, s32[1,1024]{1,0:T(1,128)} %bitcast.20, s32[1,1024]{1,0:T(1,128)} %bitcast.21, s32[1,256]{1,0:T(1,128)} %bitcast.22, s32[27,1024]{1,0:T(8,128)} %refs_3_.1, ...), custom_call_target="tpu_custom_call" | custom-call | tf_op jit(solution)/shard_map/pallas_call | solution.py:399
  36.2 2.2 %shard_map.113 = (bf16[64,1024]{1,0:T(8,128)(2,1)}, f32[27,64,64]{2,1,0:T(8,128)}, f32[512,128]{1,0:T(8,128)}) custom-call(bf16[64,1024]{1,0:T(8,128)(2,1)} %get-tuple-element.9.feat_in, bf16[1024,128]{1,0:T(8,128)(2,1)} %bitcast.15, bf16[512,128]{1,0:T(8,128)(2,1)} %bitcast.18), custom_call_target="tpu_custom_call" | custom-call | tf_op jit(solution)/shard_map/pallas_call | solution.py:428
Async XLA Ops:
  0.6 0.7 %copy-start = (s32[224]{0:T(256)S(1)}, s32[224]{0:T(256)}, u32[]{:S(2)}) copy-start(s32[224]{0:T(256)} %param.15) | copy-start | bytes 2692
